TPU v7x, 32 devices: a whole 2x2x4 slice. The times are simulated.
32 devices in a mesh: blk: 8 (over z, x), slab: 4 (over y, core).
Axes of the slice: x: 2, y: 2, z: 4, core: 2. Of those that a mesh axis runs over, the one named last changes fastest.
Arguments:
- a_tiles: bfloat16 [4096, 8192], P('blk', 'slab'), may hold values from -0.125 to 0.125
- tile_cols: int32 [16, 4, 8], P('blk', 'slab'), may hold values from 0 to 15, as said below
- tile_counts: int32 [16, 4], P('blk', 'slab'), may hold values from 1 to 8, as said below
- scaling: float32 [16384], P('slab'), may hold values from 0.1 to 10
- panel: int32 [1], replicated, may hold values from 0 to 15
Outputs:
- normal_band: float32 [4096, 3, 512], P('blk', None, 'slab')
Inputs may be any that keep to these rules, and one draw needn't show every extreme that they name: `tile_cols`: the 8 column tiles listed for one row block in one slab are distinct. `tile_counts`: the largest count is 8 in every draw.
All inputs are finite; a program needn't handle non-finite values.
Results may differ from a plain program's by a relative error of at most 0.0015.
Values may be sent and summed in bfloat16 or wider, within the bound.
A program may use at most 64 MiB of HBM per device.

v0:
```python
import jax
import jax.numpy as jnp
from jax import lax
from jax.sharding import PartitionSpec as P

ridge_shift = 0.05


def from_behind(value, axis, by):
    peers = lax.axis_size(axis)
    return lax.ppermute(value, axis, [(i, (i + by) % peers) for i in range(peers)])


def body(a_tiles, tile_cols, tile_counts, scaling, panel):
    group_rows = a_tiles.shape[0]
    blocks_here = tile_cols.shape[0]
    slot_count = tile_cols.shape[2]
    tile_size = group_rows // blocks_here
    col_tiles = scaling.shape[0] // tile_size
    slab_count = lax.axis_size("slab")
    group_pos = lax.axis_index("blk")
    slab_pos = lax.axis_index("slab")
    local_width = group_rows // slab_count
    own_cols = tile_cols[:, 0, :]
    own_counts = tile_counts[:, 0]
    slot_ids = jnp.arange(slot_count, dtype=jnp.int32)
    live = slot_ids[None, :] < own_counts[:, None]
    picked = scaling.reshape(col_tiles, tile_size)[own_cols]
    picked = jnp.where(live[..., None], picked, jnp.float32(0.0))
    own_tiles = a_tiles.reshape(blocks_here, tile_size, slot_count, tile_size)
    scaled = (own_tiles.astype(jnp.float32) * picked[:, None]).astype(jnp.bfloat16)
    flat_scaled = scaled.reshape(blocks_here, tile_size, slot_count * tile_size)

    def visit_group(tile_data, col_list, count_list):
        matches = (col_list[:, 0, :, None] == jnp.arange(col_tiles, dtype=jnp.int32)) & (
            slot_ids[None, :] < count_list[:, 0][:, None]
        )[..., None]
        found = jnp.any(matches, axis=1).astype(jnp.int32)
        lookup = jnp.sum(jnp.where(matches, slot_ids[None, :, None], 0), axis=1) + slot_count * (
            1 - found
        )
        slot_index = lookup[:, own_cols.reshape(-1)]
        visiting = tile_data.reshape(blocks_here, tile_size, slot_count, tile_size)
        padded = jnp.concatenate(
            [visiting, jnp.zeros((blocks_here, tile_size, 1, tile_size), jnp.bfloat16)], axis=2
        )
        columns = []
        for other_block in range(blocks_here):
            gathered = jnp.take(padded[other_block], slot_index[other_block], axis=1)
            gathered = gathered.reshape(tile_size, blocks_here, slot_count * tile_size)
            product = jnp.einsum(
                "axk,zak->axz", flat_scaled, gathered, preferred_element_type=jnp.float32
            )
            columns.append(product.reshape(group_rows, tile_size))
        return jnp.concatenate(columns, axis=1)

    payload = (a_tiles, tile_cols, tile_counts)
    planes = [visit_group(a_tiles, tile_cols, tile_counts)]
    moving = payload
    for repeat in range(2):
        moving = from_behind((moving[0], moving[1], moving[2]), "blk", 1)
        planes.append(visit_group(moving[0], moving[1], moving[2]))
    partial_band = jnp.stack(planes, axis=1)
    normal_rows = lax.psum_scatter(partial_band, "slab", scatter_dimension=2, tiled=True)
    row_ids = jnp.arange(group_rows, dtype=jnp.int32)
    col_ids = slab_pos * local_width + jnp.arange(local_width, dtype=jnp.int32)
    ridge_add = jnp.where(
        row_ids[:, None] == col_ids[None, :], jnp.float32(ridge_shift), jnp.float32(0.0)
    )
    plane_zero = normal_rows[:, 0, :] + ridge_add
    plane_one = normal_rows[:, 1, :]
    plane_two = normal_rows[:, 2, :]
    pivot_block = panel[0]
    pivot_group = pivot_block // blocks_here
    pivot_pos = pivot_block % blocks_here
    holds_column = group_pos == pivot_group
    panel_cols = (
        pivot_pos * tile_size + jnp.arange(tile_size, dtype=jnp.int32) - slab_pos * local_width
    )
    panel_inside = (panel_cols >= 0) & (panel_cols < local_width)
    taken = jnp.take(plane_zero, jnp.clip(panel_cols, 0, local_width - 1), axis=1)
    panel_piece = jnp.where(holds_column & panel_inside[None, :], taken, jnp.float32(0.0))
    panel_column = lax.psum(panel_piece, "slab")
    pivot_tile = lax.dynamic_slice(
        panel_column, (pivot_pos * tile_size, jnp.int32(0)), (tile_size, tile_size)
    )
    identity = jnp.eye(tile_size, dtype=jnp.float32)
    pivot_tile = jnp.where(holds_column, pivot_tile, identity)
    factor = jnp.linalg.cholesky(pivot_tile)
    solved_own = jax.scipy.linalg.solve_triangular(factor, panel_column.T, lower=True).T
    row_blocks = row_ids // tile_size
    is_pivot = row_blocks == pivot_pos
    mask_own = holds_column & jnp.logical_not(is_pivot)
    lower_own = jnp.where(mask_own[:, None], solved_own, jnp.float32(0.0))
    plane_zero = plane_zero - jnp.dot(
        lower_own,
        lower_own[col_ids].T,
        precision=lax.Precision.HIGHEST,
        preferred_element_type=jnp.float32,
    )
    stacked_factor = jnp.tile(factor, (blocks_here, 1))
    new_column = jnp.where(is_pivot[:, None], stacked_factor, solved_own)
    within_panel = col_ids - pivot_pos * tile_size
    column_ok = (within_panel >= 0) & (within_panel < tile_size)
    new_values = jnp.take(new_column, jnp.clip(within_panel, 0, tile_size - 1), axis=1)
    replace_here = column_ok[None, :] & holds_column
    plane_zero = jnp.where(replace_here, new_values, plane_zero)
    return jnp.stack([plane_zero, plane_one, plane_two], axis=1)


def solution(mesh):
    return jax.shard_map(
        body,
        mesh=mesh,
        in_specs=(P("blk", "slab"), P("blk", "slab", None), P("blk", "slab"), P("slab"), P()),
        out_specs=P("blk", None, "slab"),
        check_vma=False,
    )
```

profile of v0, /device:TPU:0, one launch (start us, length us, event | category | flops | bytes accessed | tf_op | source)
XLA Modules:
  0.0 289.4 jit_solution(5105207143155115110)
XLA Ops:
  6.5 2.9 %collective-permute-start.1 = (s32[2,1,8]{2,1,0:T(1,128)}, s32[2,1,8]{2,1,0:T(1,128)S(1)}, u32[]{:S(2)}, u32[]{:S(2)}) collective-permute-start(s32[2,1,8]{2,1,0:T(1,128)} %param.8), channel_id=1, source_target_pairs={{0,4},{4,8},{8,12},{12,16},{16,20},{20,24},{24,28},{28,0},{1,5},{5... | collective-permute-start | bytes 200 | tf_op jit(solution)/shard_map/ppermute | solution.py:11
  19.8 2.3 copy.104
  26.6 2.4 copy.76
  31.3 4.1 %copy.78 = bf16[256,16,256]{0,2,1:T(8,128)(2,1)} copy(bf16[256,16,256]{2,0,1:T(8,128)(2,1)} %select_bitcast_fusion.4) | data formatting | bytes 4194304 | tf_op jit(solution)/shard_map/jit(_take)/select_n | solution.py:49
  35.4 2.4 fusion.19
  41.4 19.5 %collective-permute-done.5 = s32[2,1]{0,1:T(1,128)S(1)} collective-permute-done((s32[2,1]{0,1:T(1,128)S(1)}, s32[2,1]{0,1:T(1,128)S(1)}, u32[]{:S(2)}, u32[]{:S(2)}) %collective-permute-start.5) | collective-permute-done | bytes 40 | tf_op jit(solution)/shard_map/ppermute | solution.py:11
  62.1 6.0 %collective-permute-done.4 = s32[2,1,8]{2,1,0:T(1,128)S(1)} collective-permute-done((s32[2,1,8]{2,1,0:T(1,128)S(1)}, s32[2,1,8]{2,1,0:T(1,128)S(1)}, u32[]{:S(2)}, u32[]{:S(2)}) %collective-permute-start.4) | collective-permute-done | bytes 96 | tf_op jit(solution)/shard_map/ppermute | solution.py:11
  69.4 2.3 copy.105
  76.3 2.4 copy.82
  81.0 4.1 %copy.84 = bf16[256,16,256]{0,2,1:T(8,128)(2,1)} copy(bf16[256,16,256]{2,0,1:T(8,128)(2,1)} %select_bitcast_fusion.2) | data formatting | bytes 4194304 | tf_op jit(solution)/shard_map/jit(_take)/select_n | solution.py:49
  85.1 2.4 fusion.15
  89.5 27.7 %collective-permute-done.3 = bf16[512,2048]{1,0:T(8,128)(2,1)} collective-permute-done((bf16[512,2048]{1,0:T(8,128)(2,1)}, bf16[512,2048]{1,0:T(8,128)(2,1)}, u32[]{:S(2)}, u32[]{:S(2)}) %collective-permute-start.3) | collective-permute-done | bytes 2097184 | tf_op jit(solution)/shard_map/ppermute | solution.py:11
  117.1 2.3 copy.106
  124.0 2.4 copy.88
  126.4 3.7 %fusion.11 = f32[2,256,256]{2,1,0:T(8,128)} fusion(bf16[256,2,2048]{0,2,1:T(8,128)(2,1)} %bitcast.159, bf16[2,256,2048]{2,1,0:T(8,128)(2,1)} %bitcast.148, f32[2,2048]{1,0:T(2,128)S(1)} %bitcast.177), kind=kOutput, calls=%fused_computation.45 | convolution fusion | flops 540016640 | bytes 4734976 | tf_op jit(solution)/shard_map/axk,zak->axz/dot_general | solution.py:51
  132.4 4.1 %copy.90 = bf16[256,16,256]{0,2,1:T(8,128)(2,1)} copy(bf16[256,16,256]{2,0,1:T(8,128)(2,1)} %select_bitcast_fusion) | data formatting | bytes 4194304 | tf_op jit(solution)/shard_map/jit(_take)/select_n | solution.py:49
  136.5 2.4 fusion.9
  143.4 34.3 %reduce-scatter.2.cloned.1.call-done = f32[512,3,128]{2,0,1:T(8,128)} async-done(((f32[512,3,512]{2,0,1:T(8,128)}), f32[512,3,128]{2,0,1:T(8,128)}) %reduce-scatter.2.cloned.1.call-update) | async-done | bytes 786448 | tf_op jit(solution)/shard_map/reduce_scatter | solution.py:64
  180.9 33.3 %all-reduce.6.cloned.1.call-done = f32[512,256]{0,1:T(8,128)} async-done(((f32[512,256]{0,1:T(8,128)}), f32[512,256]{0,1:T(8,128)}) %all-reduce.6.cloned.1.call-update) | async-done | bytes 524304 | tf_op jit(solution)/shard_map/psum | solution.py:83
  216.4 11.7 %cholesky.50 = f32[128,128]{1,0:T(8,128)S(1)} custom-call(f32[128,128]{1,0:T(8,128)S(1)} %cholesky.118), custom_call_target="Cholesky" | custom-call | tf_op jit(solution)/shard_map/jit(cholesky)/cholesky | solution.py:89
  228.1 9.8 %custom-call.15 = f32[1,128,128]{1,2,0:T(8,128)S(1)} custom-call(f32[1,128,128]{2,1,0:T(8,128)S(1)} %get-tuple-element.43), custom_call_target="InvertDiagBlocksLowerTriangular" | custom-call | tf_op jit(solution)/shard_map/jit(cholesky)/cholesky | solution.py:89
  238.4 11.7 %cholesky.105 = f32[128,128]{1,0:T(8,128)S(1)} custom-call(f32[128,128]{1,0:T(8,128)S(1)} %convolution_subtract_fusion.2), custom_call_target="Cholesky" | custom-call | tf_op jit(solution)/shard_map/jit(cholesky)/cholesky | solution.py:89
  253.0 4.3 %while.1 = (s32[]{:T(128)}, f32[256,256]{1,0:T(8,128)S(1)}, s32[2,2]{1,0:T(2,128)S(1)}, f32[2,128,128]{2,1,0:T(8,128)S(1)}, s32[]{:T(128)}) while((s32[]{:T(128)}, f32[256,256]{1,0:T(8,128)S(1)}, s32[2,2]{1,0:T(2,128)S(1)}, f32[2,128,128]{2,1,0:T(8,128)S(1)}, s32[]{:T(128)}) %tuple.41), condition=%wide.while_cond, body=%wide.while_body.sunk | while | flops 2 | bytes 131181 | solution.py:90
  257.3 19.7 %custom-call.16 = f32[2,128,128]{1,2,0:T(8,128)S(1)} custom-call(f32[2,128,128]{2,1,0:T(8,128)S(1)} %get-tuple-element.13), custom_call_target="InvertDiagBlocksLowerTriangular" | custom-call | tf_op jit(solution)/shard_map/jit(_solve_triangular)/triangular_solve | solution.py:90
  (148 shorter events, 59.2 us)
Async XLA Ops:
  6.5 171.2 %reduce-scatter.2.cloned.1.call-start = ((), (), s32[]{:S(2)}) async-start(), calls=%async_computation.1 | async-start | bytes 3932160 | tf_op jit(solution)/shard_map/reduce_scatter | solution.py:64
  6.5 54.4 %collective-permute-start.1 = (s32[2,1,8]{2,1,0:T(1,128)}, s32[2,1,8]{2,1,0:T(1,128)S(1)}, u32[]{:S(2)}, u32[]{:S(2)}) collective-permute-start(s32[2,1,8]{2,1,0:T(1,128)} %param.8), channel_id=1, source_target_pairs={{0,4},{4,8},{8,12},{12,16},{16,20},{20,24},{24,28},{28,0},{1,5},{5... | collective-permute-start | bytes 200 | tf_op jit(solution)/shard_map/ppermute | solution.py:11
  9.5 30.3 %collective-permute-start.2 = (s32[2,1]{0,1:T(1,128)}, s32[2,1]{0,1:T(1,128)S(1)}, u32[]{:S(2)}, u32[]{:S(2)}) collective-permute-start(s32[2,1]{0,1:T(1,128)} %param.9), channel_id=1, source_target_pairs={{0,4},{4,8},{8,12},{12,16},{16,20},{20,24},{24,28},{28,0},{1,5},{5... | collective-permute-start | bytes 32 | tf_op jit(solution)/shard_map/ppermute | solution.py:11
  11.0 58.1 %collective-permute-start = (bf16[512,2048]{1,0:T(8,128)(2,1)}, bf16[512,2048]{1,0:T(8,128)(2,1)}, u32[]{:S(2)}, u32[]{:S(2)}) collective-permute-start(bf16[512,2048]{1,0:T(8,128)(2,1)} %param.7), channel_id=1, source_target_pairs={{0,4},{4,8},{8,12},{12,16},{16,20},{20,24},{24,28},{28,0},{1,5},{5... | collective-permute-start | bytes 6291464 | tf_op jit(solution)/shard_map/ppermute | solution.py:11
  31.3 4.1 %copy-start.2 = (bf16[512,2048]{1,0:T(8,128)(2,1)S(1)}, bf16[512,2048]{1,0:T(8,128)(2,1)}, u32[]{:S(2)}) copy-start(bf16[512,2048]{1,0:T(8,128)(2,1)} %param.7) | copy-start | bytes 6291460
  35.4 2.5 copy-start.5
  39.8 21.0 %collective-permute-start.5 = (s32[2,1]{0,1:T(1,128)S(1)}, s32[2,1]{0,1:T(1,128)S(1)}, u32[]{:S(2)}, u32[]{:S(2)}) collective-permute-start(s32[2,1]{0,1:T(1,128)S(1)} %collective-permute-done.2), channel_id=1, source_target_pairs={{0,4},{4,8},{8,12},{12,16},{16,20},{20,24},{24,28},{28,0},{1,5},{5... | collective-permute-start | bytes 32 | tf_op jit(solution)/shard_map/ppermute | solution.py:11
  61.8 6.3 %collective-permute-start.4 = (s32[2,1,8]{2,1,0:T(1,128)S(1)}, s32[2,1,8]{2,1,0:T(1,128)S(1)}, u32[]{:S(2)}, u32[]{:S(2)}) collective-permute-start(s32[2,1,8]{2,1,0:T(1,128)S(1)} %collective-permute-done.1), channel_id=1, source_target_pairs={{0,4},{4,8},{8,12},{12,16},{16,20},{20,24},{24,28},{28,0},{1,5},{5... | collective-permute-start | bytes 200 | tf_op jit(solution)/shard_map/ppermute | solution.py:11
  69.1 48.0 %collective-permute-start.3 = (bf16[512,2048]{1,0:T(8,128)(2,1)}, bf16[512,2048]{1,0:T(8,128)(2,1)}, u32[]{:S(2)}, u32[]{:S(2)}) collective-permute-start(bf16[512,2048]{1,0:T(8,128)(2,1)} %collective-permute-done), channel_id=1, source_target_pairs={{0,4},{4,8},{8,12},{12,16},{16,20},{20,24},{24,28},{28,0},{1,5},{5... | collective-permute-start | bytes 6291464 | tf_op jit(solution)/shard_map/ppermute | solution.py:11
  81.0 4.1 %copy-start.3 = (bf16[512,2048]{1,0:T(8,128)(2,1)S(1)}, bf16[512,2048]{1,0:T(8,128)(2,1)}, u32[]{:S(2)}) copy-start(bf16[512,2048]{1,0:T(8,128)(2,1)} %param.7) | copy-start | bytes 6291460
  85.1 2.5 copy-start.6
  132.4 4.1 %copy-start.4 = (bf16[512,2048]{1,0:T(8,128)(2,1)S(1)}, bf16[512,2048]{1,0:T(8,128)(2,1)}, u32[]{:S(2)}) copy-start(bf16[512,2048]{1,0:T(8,128)(2,1)} %param.7) | copy-start | bytes 6291460
  136.5 2.4 copy-start.8
  138.8 1.2 copy-start
  138.9 1.5 copy-start.1
  142.4 71.8 %all-reduce.6.cloned.1.call-start = ((), (), s32[]{:S(2)}) async-start(), calls=%async_computation.2 | async-start | bytes 1048576 | tf_op jit(solution)/shard_map/psum | solution.py:83
  215.2 61.8 %copy-start.7 = (f32[512,256]{0,1:T(8,128)S(1)}, f32[512,256]{0,1:T(8,128)}, u32[]{:S(2)}) copy-start(f32[512,256]{0,1:T(8,128)} %all-reduce.6.cloned.1.call-done) | copy-start | bytes 1572868
  279.7 1.9 slice-start
Sparse Core Ops, SparseCore 0:
  142.5 35.2 reduce-scatter.1
  181.0 33.1 all-reduce.5
where the time goes:
time: 290 us; the launch traced here: 289 us
  waiting for transfers between devices  121 us (42%)
  other arithmetic  79.2 us (27%)
  local copies, waits for them, and re-layouts  49.8 us (17%)
  between operations  16 us (6%)
  matrix products  15.2 us (5%)
  starting transfers between devices  8.09 us (3%)
    ppermute x6, waiting for transfers between devices, from_behind(): lax.ppermute(value, axis, [(i, (i + by) % peers) for i in range(peers)])  53.2 us
    another operation x7, other arithmetic, body(): factor = jnp.linalg.cholesky(pivot_tile)  34.7 us
    reduce_scatter x1, waiting for transfers between devices, body(): lax.psum_scatter(partial_band, 'slab', scatter_dimension=2, tiled=True)  34.3 us
    psum x1, waiting for transfers between devices, body(): panel_column = lax.psum(panel_piece, 'slab')  33.3 us
    another operation x3, other arithmetic, body(): jax.scipy.linalg.solve_triangular(factor, panel_column.T, lower=True)  19.7 us
    select_n x6, local copies, waits for them, and re-layouts, visit_group(): gathered = jnp.take(padded[other_block], slot_index[other_block], axis=1)  19.4 us
    dot_general x6, matrix products, visit_group(): jnp.einsum('axk,zak->axz', flat_scaled, gathered, preferred_element_type=...  12.5 us
    select_n x9, other arithmetic, visit_group(): gathered = jnp.take(padded[other_block], slot_index[other_block], axis=1)  10.5 us
  transfers between devices with their start and end apart: 8, of which 5 were waited for; matrix products, arithmetic and copies ran while one was open for 17% of the time, Pallas kernels for 0%

commit v1 on v0

v1 whole, which is shorter than its diff:
```python
import functools

import jax
import jax.numpy as jnp
from jax import lax
from jax.experimental import pallas as pl
from jax.experimental.pallas import tpu as pltpu
from jax.sharding import PartitionSpec as P

ridge_shift = 0.05
MESH = pl.DeviceIdType.MESH
PIECES = 8


def band_kernel(
    groups, slots, a_ref, picked_ref, meta_ref, pos_ref, band_ref, column_ref,
    scaled, aligned, one_far, one_near, two_far, two_near, meta_one, meta_two, part, landed, gathered,
    z_send, z_recv, x_send, x_recv, meta_send, meta_recv,
    sum_send, sum_recv, all_send, all_recv,
):
    rows = a_ref.shape[0]
    tile = rows // 2
    half = tile // 2
    piece = rows // PIECES
    per_block = PIECES // 2
    group = lax.axis_index("blk")
    slab = lax.axis_index("slab")
    chip = slab // 2
    core = slab % 2
    odd = group % 2
    ahead = (group + 2) % groups
    behind = (group + groups - 2) % groups
    across = group + 1 - 2 * odd
    mate = chip * 2 + 1 - core
    facing = (1 - chip) * 2 + core
    diagonal = (1 - chip) * 2 + 1 - core
    peers = (mate, facing, diagonal)
    far = 1 - chip
    near = chip

    barrier = pltpu.get_barrier_semaphore()
    for other in (ahead, behind, across):
        pl.semaphore_signal(barrier, inc=1, device_id=(other, slab), device_id_type=MESH)
    for other in peers:
        pl.semaphore_signal(barrier, inc=1, device_id=(group, other), device_id_type=MESH)
    pl.semaphore_wait(barrier, 6)

    def piece_rows(n):
        block = far if n < per_block else near
        return pl.ds(pl.multiple_of(block * tile + (n % per_block) * piece, piece), piece)

    def piece_of(far_ref, near_ref, n):
        start = n % per_block * piece
        return (far_ref if n < per_block else near_ref).at[start:start + piece]

    def to_ahead(n):
        return pltpu.make_async_remote_copy(
            src_ref=a_ref.at[piece_rows(n)], dst_ref=piece_of(two_far, two_near, n),
            send_sem=z_send.at[n], recv_sem=z_recv.at[n],
            device_id=(ahead, slab), device_id_type=MESH)

    def to_across(n, source):
        return pltpu.make_async_remote_copy(
            src_ref=source, dst_ref=piece_of(one_far, one_near, n),
            send_sem=x_send.at[n], recv_sem=x_recv.at[n],
            device_id=(across, slab), device_id_type=MESH)

    def meta_ahead():
        return pltpu.make_async_remote_copy(
            src_ref=meta_ref, dst_ref=meta_two, send_sem=meta_send.at[0], recv_sem=meta_recv.at[0],
            device_id=(ahead, slab), device_id_type=MESH)

    def meta_across(source):
        return pltpu.make_async_remote_copy(
            src_ref=source, dst_ref=meta_one, send_sem=meta_send.at[1], recv_sem=meta_recv.at[1],
            device_id=(across, slab), device_id_type=MESH)

    meta_ahead().start()
    for n in range(PIECES):
        to_ahead(n).start()

    @pl.when(odd == 0)
    def _():
        meta_across(meta_ref).start()
        for n in range(PIECES):
            to_across(n, a_ref.at[piece_rows(n)]).start()

    def scale_slot(i, m):
        where = (pl.ds(i * tile, tile), pl.ds(m * tile, tile))
        factors = picked_ref[i * slots + m:i * slots + m + 1, :]
        scaled[where] = (a_ref[where].astype(jnp.float32) * factors).astype(jnp.bfloat16)

    for i in range(2):
        for m in range(slots):
            scale_slot(i, m)

    def sum_copy(plane, d):
        return pltpu.make_async_remote_copy(
            src_ref=part.at[plane, peers[d]], dst_ref=landed.at[plane, d],
            send_sem=sum_send.at[plane, d], recv_sem=sum_recv.at[plane, d],
            device_id=(group, peers[d]), device_id_type=MESH)

    def multiply(plane, block, source, other_meta):
        first = pl.ds(0, tile)
        if plane == 0:
            first = pl.ds(pl.multiple_of(block * tile, tile), tile)

        def align(i):
            def one_slot(m, carry):
                mine = meta_ref[pl.ds(i * slots + m, 1), :]
                total = jnp.zeros((tile, tile), jnp.bfloat16)
                for n in range(slots):
                    theirs = other_meta[pl.ds(block * slots + n, 1), :]
                    same = jnp.where(mine == theirs, jnp.float32(1.0), jnp.float32(0.0))
                    same = jnp.concatenate([same, same], axis=1).astype(jnp.bfloat16)
                    total += source[first, n * tile:(n + 1) * tile] * same
                aligned[:, pl.ds(pl.multiple_of(m * tile, tile), tile)] = total
                return carry

            lax.fori_loop(0, slots, one_slot, 0)
            return aligned[...]

        def one(i, direct):
            here = pl.ds(pl.multiple_of(i * tile, tile), tile)
            other = source[first, :] if direct else align(i)
            total = lax.dot_general(
                scaled[here, :], other, (((1,), (1,)), ((), ())),
                preferred_element_type=jnp.float32)
            part[plane, 2 * block, here] = total[:, :half]
            part[plane, 2 * block + 1, here] = total[:, half:]

        one(block, plane == 0)
        one(1 - block, False)
        if block is far:
            sum_copy(plane, 1).start()
            sum_copy(plane, 2).start()
        else:
            sum_copy(plane, 0).start()

    def forward(n):
        to_ahead(n).wait_recv()

        @pl.when(odd == 1)
        def _():
            to_across(n, piece_of(two_far, two_near, n)).start()

    multiply(0, far, a_ref, meta_ref)
    multiply(0, near, a_ref, meta_ref)

    meta_ahead().wait_recv()

    @pl.when(odd == 1)
    def _():
        meta_across(meta_two).start()

    forward(0)
    meta_across(meta_ref).wait_recv()

    for d in range(3):
        sum_copy(0, d).wait_recv()
    row_ids = lax.broadcasted_iota(jnp.int32, (rows, half), 0)
    col_ids = lax.broadcasted_iota(jnp.int32, (rows, half), 1) + slab * half
    ridge = jnp.where(row_ids == col_ids, jnp.float32(ridge_shift), jnp.float32(0.0))
    gathered[slab] = (part[0, slab] + landed[0, 0]) + (landed[0, 1] + landed[0, 2]) + ridge

    def all_copy(d):
        return pltpu.make_async_remote_copy(
            src_ref=gathered.at[slab], dst_ref=gathered.at[slab],
            send_sem=all_send.at[d], recv_sem=all_recv.at[d],
            device_id=(group, peers[d]), device_id_type=MESH)

    def all_arrival(d):
        return pltpu.make_async_remote_copy(
            src_ref=gathered.at[slab], dst_ref=gathered.at[peers[d]],
            send_sem=all_send.at[d], recv_sem=all_recv.at[d],
            device_id=(group, peers[d]), device_id_type=MESH)

    for d in (1, 2, 0):
        all_copy(d).start()
    band_ref[0] = gathered[slab]

    for n in range(1, per_block):
        forward(n)
    multiply(2, far, two_far, meta_two)
    for n in range(per_block):
        to_across(n, piece_of(two_far, two_near, n)).wait_recv()
    multiply(1, far, one_far, meta_one)

    for d in range(3):
        all_arrival(d).wait_recv()
    first_half = pos_ref[0:1, :] == 0
    for h in range(2):
        column_ref[:, h * half:(h + 1) * half] = jnp.where(
            first_half, gathered[h], gathered[2 + h])

    for n in range(per_block, PIECES):
        forward(n)
    multiply(2, near, two_near, meta_two)
    for n in range(per_block, PIECES):
        to_across(n, piece_of(two_far, two_near, n)).wait_recv()
    multiply(1, near, one_near, meta_one)
    for plane in (2, 1):
        for d in range(3):
            sum_copy(plane, d).wait_recv()
        band_ref[plane] = (part[plane, slab] + landed[plane, 0]) + (
            landed[plane, 1] + landed[plane, 2])

    meta_ahead().wait_send()
    meta_across(meta_ref).wait_send()
    for n in range(PIECES):
        to_ahead(n).wait_send()
        to_across(n, piece_of(two_far, two_near, n)).wait_send()
    for d in range(3):
        all_copy(d).wait_send()
        for plane in range(3):
            sum_copy(plane, d).wait_send()


def body(a_tiles, tile_cols, tile_counts, scaling, panel):
    rows = a_tiles.shape[0]
    blocks_here = tile_cols.shape[0]
    slots = tile_cols.shape[2]
    tile = rows // blocks_here
    half = rows // 4
    col_tiles = scaling.shape[0] // tile
    groups = lax.axis_size("blk")
    group_pos = lax.axis_index("blk")
    slab_pos = lax.axis_index("slab")
    cols = tile_cols[:, 0, :]
    slot_ids = jnp.arange(slots, dtype=jnp.int32)
    live = slot_ids[None, :] < tile_counts
    picked = jnp.where(live[..., None], scaling.reshape(col_tiles, tile)[cols], jnp.float32(0.0))
    picked = picked.reshape(blocks_here * slots, tile)
    meta = jnp.where(live, cols, -1).reshape(blocks_here * slots, 1)
    meta = jnp.broadcast_to(meta, (blocks_here * slots, half))
    positions = jnp.full((8, half), panel[0] % blocks_here, jnp.int32)
    vmem = pl.BlockSpec(memory_space=pltpu.VMEM)
    dma = pltpu.SemaphoreType.DMA
    band, column = pl.pallas_call(
        functools.partial(band_kernel, groups, slots),
        out_shape=(
            jax.ShapeDtypeStruct((3, rows, half), jnp.float32),
            jax.ShapeDtypeStruct((rows, tile), jnp.float32),
        ),
        in_specs=[vmem] * 4,
        out_specs=(vmem, vmem),
        scratch_shapes=[
            pltpu.VMEM(a_tiles.shape, jnp.bfloat16),
            pltpu.VMEM((tile, slots * tile), jnp.bfloat16),
            *[pltpu.VMEM((tile, slots * tile), jnp.bfloat16)] * 4,
            *[pltpu.VMEM((blocks_here * slots, half), jnp.int32)] * 2,
            pltpu.VMEM((3, 4, rows, half), jnp.float32),
            pltpu.VMEM((3, 3, rows, half), jnp.float32),
            pltpu.VMEM((4, rows, half), jnp.float32),
            dma((PIECES,)), dma((PIECES,)), dma((PIECES,)), dma((PIECES,)),
            dma((2,)), dma((2,)),
            dma((3, 3)), dma((3, 3)), dma((3,)), dma((3,)),
        ],
        compiler_params=pltpu.CompilerParams(
            collective_id=0, has_side_effects=True, vmem_limit_bytes=40 * 2**20),
        name="band",
    )(a_tiles, picked, meta, positions)

    row_ids = jnp.arange(rows, dtype=jnp.int32)
    pivot_block = panel[0]
    pos = pivot_block % blocks_here
    holds = group_pos == pivot_block // blocks_here
    pivot_tile = jnp.where(pos == 0, column[:tile], column[tile:])
    other_tile = jnp.where(pos == 0, column[tile:], column[:tile])
    pivot_tile = jnp.where(holds, pivot_tile, jnp.eye(tile, dtype=jnp.float32))
    factor = jnp.linalg.cholesky(pivot_tile)
    solved = lax.linalg.triangular_solve(
        factor, other_tile, left_side=False, lower=True, transpose_a=True)
    here = slab_pos % 2
    pick = lambda m, axis: lax.dynamic_slice_in_dim(m, here * half, half, axis)
    reduced = jnp.dot(
        solved, pick(solved, 0).T, precision=lax.Precision.HIGHEST,
        preferred_element_type=jnp.float32)
    in_panel = slab_pos // 2 == pos
    top = jnp.where(pos == 0, pick(factor, 1), pick(solved, 1))
    low = jnp.where(pos == 0, pick(solved, 1), pick(factor, 1))
    plane_zero = band[0]
    replaced = jnp.concatenate([top, low], axis=0)
    zero = jnp.zeros_like(reduced)
    lessened = plane_zero - jnp.concatenate(
        [jnp.where(pos == 0, zero, reduced), jnp.where(pos == 0, reduced, zero)], axis=0)
    updated = jnp.where(in_panel, replaced, lessened)
    plane_zero = jnp.where(holds, updated, plane_zero)
    return jnp.stack([plane_zero, band[1], band[2]], axis=1)


def solution(mesh):
    return jax.shard_map(
        body,
        mesh=mesh,
        in_specs=(P("blk", "slab"), P("blk", "slab", None), P("blk", "slab"), P("slab"), P()),
        out_specs=P("blk", None, "slab"),
        check_vma=False,
    )
```

time: 290 us -> 138 us (0.48)
  waiting for transfers between devices: 121 us -> 0 us
  Pallas kernels: 0 us -> 66.6 us
  local copies, waits for them, and re-layouts: 49.8 us -> 8.3 us
  other arithmetic: 79.2 us -> 58.5 us
  between operations: 16 us -> 2.27 us
  matrix products: 15.2 us -> 1.85 us
  starting transfers between devices: 8.09 us -> 0 us
    pallas_call x0 -> x1, Pallas kernels: none -> 66.6 us  [body(): pl.pallas_call(functools.partial(band_kernel, groups, slots), out_shape=(...]
    ppermute x6 -> x0, waiting for transfers between devices: 53.2 us -> none  [from_behind(): lax.ppermute(value, axis, [(i, (i + by) % peers) for i in range(peers)])]
    reduce_scatter x1 -> x0, waiting for transfers between devices: 34.3 us -> none  [body(): lax.psum_scatter(partial_band, 'slab', scatter_dimension=2, tiled=True)]
    psum x1 -> x0, waiting for transfers between devices: 33.3 us -> none  [body(): panel_column = lax.psum(panel_piece, 'slab')]
    select_n x10 -> x2, local copies, waits for them, and re-layouts: 20 us -> 0.21 us  [the longest x1 0.13 us: body(): pivot_tile = jnp.where(holds, pivot_tile, jnp.eye(tile, dtype=jnp.float32))]
    dot_general x7 -> x1, matrix products: 13.5 us -> 0.41 us  [body(): jnp.dot(solved, pick(solved, 0).T, precision=lax.Precision.HIGHEST, prefe...]
    gather x14 -> x1, local copies, waits for them, and re-layouts: 12.9 us -> 0.57 us  [body(): scaling.reshape(col_tiles, tile)[cols]]
    select_n x16 -> x5, other arithmetic: 13.2 us -> 0.85 us  [the longest x1 0.68 us: body(): scaling.reshape(col_tiles, tile)[cols]]
  transfers between devices with their start and end apart: 8 -> 0, of which waited for: 5 -> 0; matrix products, arithmetic and copies ran while one was open for 17% -> 0% of each run, Pallas kernels for 0% -> 0%
where the time goes in v1:
time: 138 us
  Pallas kernels  66.6 us (48%)
  other arithmetic  58.5 us (42%)
  local copies, waits for them, and re-layouts  8.3 us (6%)
  between operations  2.27 us (2%)
  matrix products  1.85 us (1%)
    pallas_call x1, Pallas kernels, body(): pl.pallas_call(functools.partial(band_kernel, groups, slots), out_shape=(...  66.6 us
    another operation x7, other arithmetic, body(): factor = jnp.linalg.cholesky(pivot_tile)  34.7 us
    another operation x3, other arithmetic, body(): lax.linalg.triangular_solve(factor, other_tile, left_side=False, lower=Tr...  19.9 us
    another operation x6, local copies, waits for them, and re-layouts  4.02 us

profile of v1, /device:TPU:0, one launch (start us, length us, event | category | flops | bytes accessed | tf_op | source)
XLA Modules:
  0.0 137.6 jit_solution(1603585704107513737)
XLA Ops:
  0.7 0.7 iota_compare_fusion.4
  1.5 0.7 reshape.164
  2.2 0.7 compare_select_fusion
  3.0 0.6 gather_fusion
  3.6 0.5 broadcast.178
  4.2 1.3 reduce.15
  5.7 1.6 %copy-done = bf16[512,2048]{1,0:T(8,128)(2,1)S(1)} copy-done((bf16[512,2048]{1,0:T(8,128)(2,1)S(1)}, bf16[512,2048]{1,0:T(8,128)(2,1)}, u32[]{:S(2)}) %copy-start) | copy-done | bytes 2097176
  7.3 66.6 %band.1 = (f32[3,512,128]{2,1,0:T(8,128)S(1)}, f32[512,256]{1,0:T(8,128)S(1)}) custom-call(bf16[512,2048]{1,0:T(8,128)(2,1)S(1)} %copy-done, f32[16,256]{1,0:T(8,128)S(1)} %broadcast_select_fusion.picked_ref, s32[16,128]{1,0:T(8,128)S(1)} %broadcast_in_dim.35.meta_ref, s32[8,128]{1,0:T(8,128)S(1)} %broadcast_in_dim.36.pos_ref), custom_call_target="tpu_custom_call" | custom-call | tf_op jit(solution)/shard_map/band/pallas_call | solution.py:239
  74.4 11.7 %cholesky.50 = f32[128,128]{1,0:T(8,128)S(1)} custom-call(f32[128,128]{1,0:T(8,128)S(1)} %cholesky.118), custom_call_target="Cholesky" | custom-call | tf_op jit(solution)/shard_map/jit(cholesky)/cholesky | solution.py:271
  86.1 9.8 %custom-call.14 = f32[1,128,128]{1,2,0:T(8,128)S(1)} custom-call(f32[1,128,128]{2,1,0:T(8,128)S(1)} %get-tuple-element.40), custom_call_target="InvertDiagBlocksLowerTriangular" | custom-call | tf_op jit(solution)/shard_map/jit(cholesky)/cholesky | solution.py:271
  96.2 0.3 convolution_subtract_fusion.1
  96.4 11.7 %cholesky.105 = f32[128,128]{1,0:T(8,128)S(1)} custom-call(f32[128,128]{1,0:T(8,128)S(1)} %convolution_subtract_fusion.1), custom_call_target="Cholesky" | custom-call | tf_op jit(solution)/shard_map/jit(cholesky)/cholesky | solution.py:271
  108.2 0.7 compare_reduce_fusion
  108.9 0.6 compare_reduce_fusion.1
  111.0 4.1 %while.1 = (s32[]{:T(128)}, f32[256,256]{1,0:T(8,128)S(1)}, s32[2,2]{1,0:T(2,128)S(1)}, f32[2,128,128]{2,1,0:T(8,128)S(1)}, s32[]{:T(128)}) while((s32[]{:T(128)}, f32[256,256]{1,0:T(8,128)S(1)}, s32[2,2]{1,0:T(2,128)S(1)}, f32[2,128,128]{2,1,0:T(8,128)S(1)}, s32[]{:T(128)}) %tuple.29), condition=%wide.while_cond, body=%wide.while_body.sunk | while | flops 2 | bytes 131181 | solution.py:272
  111.0 0.7 fusion.24
  111.7 1.3 bitcast_dynamic-update-slice_fusion.2
  113.1 0.7 fusion.24
  113.7 1.3 bitcast_dynamic-update-slice_fusion.2
  115.1 19.9 %custom-call.15 = f32[2,128,128]{1,2,0:T(8,128)S(1)} custom-call(f32[2,128,128]{2,1,0:T(8,128)S(1)} %get-tuple-element.16), custom_call_target="InvertDiagBlocksLowerTriangular" | custom-call | tf_op jit(solution)/shard_map/triangular_solve | solution.py:272
  135.0 0.3 fusion.7
  135.6 0.4 fusion.9
  136.1 0.4 select_bitcast_fusion.1
  136.6 0.9 pad_maximum_fusion
  (28 shorter events, 1.7 us)
Async XLA Ops:
  5.7 1.6 %copy-start = (bf16[512,2048]{1,0:T(8,128)(2,1)S(1)}, bf16[512,2048]{1,0:T(8,128)(2,1)}, u32[]{:S(2)}) copy-start(bf16[512,2048]{1,0:T(8,128)(2,1)} %a_ref.1) | copy-start | bytes 6291460

commit v2 on v1

--- a/solution.py
+++ b/solution.py
@@ -10,11 +10,76 @@
 ridge_shift = 0.05
 MESH = pl.DeviceIdType.MESH
 PIECES = 8
+STRIP = 32
+
+
+def split_three(value):
+    high = value.astype(jnp.bfloat16)
+    rest = value - high.astype(jnp.float32)
+    middle = rest.astype(jnp.bfloat16)
+    low = (rest - middle.astype(jnp.float32)).astype(jnp.bfloat16)
+    return high, middle, low
+
+
+def transposed_product(left, right):
+    lh, lm, ll = split_three(left)
+    rh, rm, rl = split_three(right)
+    return lax.dot_general(
+        jnp.concatenate([ll, lm, lh, lm, lh, lh], axis=0),
+        jnp.concatenate([rh, rm, rl, rh, rm, rh], axis=0),
+        (((0,), (0,)), ((), ())), preferred_element_type=jnp.float32)
+
+
+def wide(value, times):
+    return jnp.concatenate([value] * times, axis=1)
+
+
+def factor_strip(work, upper, s):
+    size = work.shape[0]
+    width = work.shape[1]
+    times = width // 128
+    start = pl.multiple_of(s * STRIP, STRIP)
+    strip = work[pl.ds(start, STRIP), :]
+    row_ids = lax.broadcasted_iota(jnp.int32, (8, 128), 0)
+    done = []
+    rest = strip
+    for g in range(STRIP // 8):
+        lanes = lax.broadcasted_iota(jnp.int32, (rest.shape[0], size), 1)
+        square = rest[:, :size]
+        columns = []
+        for j in range(8):
+            hit = lanes == start + (8 * g + j)
+            column = jnp.sum(jnp.where(hit, square, jnp.float32(0.0)), axis=1, keepdims=True)
+            columns.append(jnp.broadcast_to(column, (rest.shape[0], 128)))
+        more = rest.shape[0] > 8
+        top, rest = rest[:8], rest[8:] if more else None
+        tops = [c[:8] for c in columns]
+        rests = [c[8:] for c in columns] if more else None
+        for j in range(8):
+            inverse = lax.rsqrt(tops[j][j:j + 1])
+            pivot_row = top[j:j + 1] * wide(inverse, times)
+            below = jnp.where(row_ids > j, tops[j] * inverse, jnp.float32(0.0))
+            top = jnp.where(wide(row_ids, times) == j, pivot_row, top - wide(below, times) * pivot_row)
+            if more:
+                lower = rests[j] * inverse
+                rest = rest - wide(lower, times) * pivot_row
+            for k in range(j + 1, 8):
+                entry = tops[k][j:j + 1] * inverse
+                tops[k] = tops[k] - below * entry
+                if more:
+                    rests[k] = rests[k] - lower * entry
+        done.append(top)
+    rows = jnp.concatenate(done, axis=0)
+    lanes = lax.broadcasted_iota(jnp.int32, rows.shape, 1)
+    own = lax.broadcasted_iota(jnp.int32, rows.shape, 0) + start
+    rows = jnp.where(lanes >= own, rows, jnp.float32(0.0))
+    upper[pl.ds(start, STRIP), :] = rows
+    work[...] -= transposed_product(rows[:, :size], rows)
 
 
 def band_kernel(
-    groups, slots, a_ref, picked_ref, meta_ref, pos_ref, band_ref, column_ref,
-    scaled, aligned, one_far, one_near, two_far, two_near, meta_one, meta_two, part, landed, gathered,
+    groups, slots, a_ref, picked_ref, meta_ref, pos_ref, band_ref,
+    scaled, aligned, one_far, one_near, two_far, two_near, meta_one, meta_two, part, landed, gathered, work, upper,
     z_send, z_recv, x_send, x_recv, meta_send, meta_recv,
     sum_send, sum_recv, all_send, all_recv,
 ):
@@ -137,6 +202,27 @@
         else:
             sum_copy(plane, 0).start()
 
+    def near_copies(n):
+        here = pl.ds(pl.multiple_of((n - per_block) * piece, piece), piece)
+        there = pl.ds(pl.multiple_of(near * tile + (n - per_block) * piece, piece), piece)
+        incoming = pltpu.make_async_remote_copy(
+            src_ref=a_ref.at[there], dst_ref=two_near.at[here],
+            send_sem=z_send.at[n], recv_sem=z_recv.at[n],
+            device_id=(ahead, slab), device_id_type=MESH)
+        outgoing = pltpu.make_async_remote_copy(
+            src_ref=two_near.at[here], dst_ref=one_near.at[here],
+            send_sem=x_send.at[n], recv_sem=x_recv.at[n],
+            device_id=(across, slab), device_id_type=MESH)
+        return incoming, outgoing
+
+    def forward_near(n):
+        incoming, outgoing = near_copies(n)
+        incoming.wait_recv()
+
+        @pl.when(odd == 1)
+        def _():
+            outgoing.start()
+
     def forward(n):
         to_ahead(n).wait_recv()
 
@@ -177,24 +263,61 @@
 
     for d in (1, 2, 0):
         all_copy(d).start()
-    band_ref[0] = gathered[slab]
 
     for n in range(1, per_block):
         forward(n)
     multiply(2, far, two_far, meta_two)
-    for n in range(per_block):
-        to_across(n, piece_of(two_far, two_near, n)).wait_recv()
-    multiply(1, far, one_far, meta_one)
-
     for d in range(3):
         all_arrival(d).wait_recv()
-    first_half = pos_ref[0:1, :] == 0
-    for h in range(2):
-        column_ref[:, h * half:(h + 1) * half] = jnp.where(
-            first_half, gathered[h], gathered[2 + h])
-
-    for n in range(per_block, PIECES):
-        forward(n)
+    pivot = pos_ref[0:1, :]
+    first = (pivot & 1) == 0
+    pivot_tile = jnp.concatenate(
+        [jnp.where(first, gathered[h, :tile], gathered[2 + h, tile:]) for h in range(2)], axis=1)
+    other_tile = jnp.concatenate(
+        [jnp.where(first, gathered[h, tile:], gathered[2 + h, :tile]) for h in range(2)], axis=1)
+    work[:, :tile] = jnp.float32(0.5) * (pivot_tile + pivot_tile.T)
+    work[:, tile:] = other_tile.T
+
+    strips = tile // STRIP
+    quarter = strips // per_block
+
+    def some_strips(n, carry):
+        def one_strip(s, carry):
+            factor_strip(work, upper, s)
+            return carry
+
+        lax.fori_loop(n * quarter, (n + 1) * quarter, one_strip, 0)
+
+        @pl.when(n < per_block - 1)
+        def _():
+            forward_near(n + per_block)
+
+        @pl.when(n == 1)
+        def _():
+            for p in range(per_block):
+                to_across(p, piece_of(two_far, two_near, p)).wait_recv()
+            multiply(1, far, one_far, meta_one)
+
+        return carry
+
+    lax.fori_loop(0, per_block, some_strips, 0)
+
+    lower_half = upper[pl.ds(pl.multiple_of(core * half, half), half), :].T
+    other_half = upper[:, pl.ds(pl.multiple_of(tile + core * half, half), half)]
+    reduced = transposed_product(upper[:, tile:], other_half)
+    top, low = gathered[slab, :tile], gathered[slab, tile:]
+    in_panel = (pivot & 1) == chip
+    holds = (pivot >> 1) == group
+    new_top = jnp.where(
+        in_panel, jnp.where(first, lower_half[:tile], lower_half[tile:]),
+        jnp.where(first, top, top - reduced))
+    new_low = jnp.where(
+        in_panel, jnp.where(first, lower_half[tile:], lower_half[:tile]),
+        jnp.where(first, low - reduced, low))
+    band_ref[0, :tile] = jnp.where(holds, new_top, top)
+    band_ref[0, tile:] = jnp.where(holds, new_low, low)
+
+    forward(PIECES - 1)
     multiply(2, near, two_near, meta_two)
     for n in range(per_block, PIECES):
         to_across(n, piece_of(two_far, two_near, n)).wait_recv()
@@ -224,8 +347,6 @@
     half = rows // 4
     col_tiles = scaling.shape[0] // tile
     groups = lax.axis_size("blk")
-    group_pos = lax.axis_index("blk")
-    slab_pos = lax.axis_index("slab")
     cols = tile_cols[:, 0, :]
     slot_ids = jnp.arange(slots, dtype=jnp.int32)
     live = slot_ids[None, :] < tile_counts
@@ -233,17 +354,14 @@
     picked = picked.reshape(blocks_here * slots, tile)
     meta = jnp.where(live, cols, -1).reshape(blocks_here * slots, 1)
     meta = jnp.broadcast_to(meta, (blocks_here * slots, half))
-    positions = jnp.full((8, half), panel[0] % blocks_here, jnp.int32)
+    positions = jnp.full((8, half), panel[0], jnp.int32)
     vmem = pl.BlockSpec(memory_space=pltpu.VMEM)
     dma = pltpu.SemaphoreType.DMA
-    band, column = pl.pallas_call(
+    band = pl.pallas_call(
         functools.partial(band_kernel, groups, slots),
-        out_shape=(
-            jax.ShapeDtypeStruct((3, rows, half), jnp.float32),
-            jax.ShapeDtypeStruct((rows, tile), jnp.float32),
-        ),
+        out_shape=jax.ShapeDtypeStruct((3, rows, half), jnp.float32),
         in_specs=[vmem] * 4,
-        out_specs=(vmem, vmem),
+        out_specs=vmem,
         scratch_shapes=[
             pltpu.VMEM(a_tiles.shape, jnp.bfloat16),
             pltpu.VMEM((tile, slots * tile), jnp.bfloat16),
@@ -252,6 +370,8 @@
             pltpu.VMEM((3, 4, rows, half), jnp.float32),
             pltpu.VMEM((3, 3, rows, half), jnp.float32),
             pltpu.VMEM((4, rows, half), jnp.float32),
+            pltpu.VMEM((tile, 2 * tile), jnp.float32),
+            pltpu.VMEM((tile, 2 * tile), jnp.float32),
             dma((PIECES,)), dma((PIECES,)), dma((PIECES,)), dma((PIECES,)),
             dma((2,)), dma((2,)),
             dma((3, 3)), dma((3, 3)), dma((3,)), dma((3,)),
@@ -261,32 +381,7 @@
         name="band",
     )(a_tiles, picked, meta, positions)
 
-    row_ids = jnp.arange(rows, dtype=jnp.int32)
-    pivot_block = panel[0]
-    pos = pivot_block % blocks_here
-    holds = group_pos == pivot_block // blocks_here
-    pivot_tile = jnp.where(pos == 0, column[:tile], column[tile:])
-    other_tile = jnp.where(pos == 0, column[tile:], column[:tile])
-    pivot_tile = jnp.where(holds, pivot_tile, jnp.eye(tile, dtype=jnp.float32))
-    factor = jnp.linalg.cholesky(pivot_tile)
-    solved = lax.linalg.triangular_solve(
-        factor, other_tile, left_side=False, lower=True, transpose_a=True)
-    here = slab_pos % 2
-    pick = lambda m, axis: lax.dynamic_slice_in_dim(m, here * half, half, axis)
-    reduced = jnp.dot(
-        solved, pick(solved, 0).T, precision=lax.Precision.HIGHEST,
-        preferred_element_type=jnp.float32)
-    in_panel = slab_pos // 2 == pos
-    top = jnp.where(pos == 0, pick(factor, 1), pick(solved, 1))
-    low = jnp.where(pos == 0, pick(solved, 1), pick(factor, 1))
-    plane_zero = band[0]
-    replaced = jnp.concatenate([top, low], axis=0)
-    zero = jnp.zeros_like(reduced)
-    lessened = plane_zero - jnp.concatenate(
-        [jnp.where(pos == 0, zero, reduced), jnp.where(pos == 0, reduced, zero)], axis=0)
-    updated = jnp.where(in_panel, replaced, lessened)
-    plane_zero = jnp.where(holds, updated, plane_zero)
-    return jnp.stack([plane_zero, band[1], band[2]], axis=1)
+    return jnp.transpose(band, (1, 0, 2))
 
 
 def solution(mesh):

time: 138 us -> 74.8 us (0.54)
  other arithmetic: 58.5 us -> 2.84 us
  local copies, waits for them, and re-layouts: 8.3 us -> 4.61 us
  matrix products: 1.85 us -> 0 us
  between operations: 2.27 us -> 0.67 us
    another operation x11 -> x0, other arithmetic: 55.5 us -> none  [the longest x7 34.7 us: body(): factor = jnp.linalg.cholesky(pivot_tile)]
    another operation x11 -> x0, local copies, waits for them, and re-layouts: 4.24 us -> none
    another operation x5 -> x0, matrix products: 1.44 us -> none  [the longest x3 0.97 us: body(): lax.linalg.triangular_solve(factor, other_tile, left_side=False, lower=Tr...]
    unnamed x3 -> x4, local copies, waits for them, and re-layouts: 2.1 us -> 2.99 us
where the time goes in v2:
time: 74.8 us; the launch traced here: 74.5 us
  Pallas kernels  66.4 us (89%)
  local copies, waits for them, and re-layouts  4.61 us (6%)
  other arithmetic  2.84 us (4%)
    pallas_call x1, Pallas kernels, body(): pl.pallas_call(functools.partial(band_kernel, groups, slots), out_shape=j...  66.4 us
    unnamed x4, local copies, waits for them, and re-layouts  2.99 us

profile of v2, /device:TPU:0, one launch (start us, length us, event | category | flops | bytes accessed | tf_op | source)
XLA Modules:
  0.0 74.5 jit_solution(10926591329089758365)
XLA Ops:
  0.7 0.7 iota_compare_fusion
  1.4 0.1 lt.40
  1.5 0.5 broadcast.53
  2.0 1.3 %reduce.3 = s32[2,8]{1,0:T(2,128)S(1)} reduce(s32[2,1,8]{2,1,0:T(1,128)} %param.6, s32[]{:T(128)} %broadcast.53), dimensions={1}, to_apply=%param.6.reduce_sub_computation.3 | reduce | bytes 132 | tf_op args[1]
  3.3 0.1 squeeze.9
  3.4 0.7 compare_select_fusion
  4.1 0.1 reshape.76
  4.2 0.1 broadcast_in_dim.30.meta_ref
  4.3 0.7 reshape.73
  5.0 0.6 gather_fusion
  5.6 0.1 broadcast_select_fusion.picked_ref
  5.6 0.0 copy-start
  5.6 1.6 %copy-done = bf16[512,2048]{1,0:T(8,128)(2,1)S(1)} copy-done((bf16[512,2048]{1,0:T(8,128)(2,1)S(1)}, bf16[512,2048]{1,0:T(8,128)(2,1)}, u32[]{:S(2)}) %copy-start) | copy-done | bytes 2097176
  7.2 66.4 %band.1 = f32[3,512,128]{2,1,0:T(8,128)S(1)} custom-call(bf16[512,2048]{1,0:T(8,128)(2,1)S(1)} %copy-done, f32[16,256]{1,0:T(8,128)S(1)} %broadcast_select_fusion.picked_ref, s32[16,128]{1,0:T(8,128)S(1)} %broadcast_in_dim.30.meta_ref, s32[8,128]{1,0:T(8,128)S(1)} %broadcast_in_dim.31.pos_ref), custom_call_target="tpu_custom_call" | custom-call | tf_op jit(solution)/shard_map/band/pallas_call | solution.py:360
  73.7 0.9 %copy.8 = f32[512,3,128]{2,0,1:T(8,128)} copy(f32[512,3,128]{2,0,1:T(8,128)S(1)} %bitcast.7) | data formatting | bytes 1572864
  (3 shorter events, 0.0 us)
Async XLA Ops:
  5.6 1.6 %copy-start = (bf16[512,2048]{1,0:T(8,128)(2,1)S(1)}, bf16[512,2048]{1,0:T(8,128)(2,1)}, u32[]{:S(2)}) copy-start(bf16[512,2048]{1,0:T(8,128)(2,1)} %a_ref.1) | copy-start | bytes 6291460

commit v3 on v2

--- a/solution.py
+++ b/solution.py
@@ -9,7 +9,7 @@
 
 ridge_shift = 0.05
 MESH = pl.DeviceIdType.MESH
-PIECES = 8
+PIECES = 9
 STRIP = 32
 
 
@@ -78,16 +78,21 @@
 
 
 def band_kernel(
-    groups, slots, a_ref, picked_ref, meta_ref, pos_ref, band_ref,
-    scaled, aligned, one_far, one_near, two_far, two_near, meta_one, meta_two, part, landed, gathered, work, upper,
-    z_send, z_recv, x_send, x_recv, meta_send, meta_recv,
+    groups, slots, a_ref, cols_ref, counts_ref, scal_ref, panel_ref, band_ref,
+    own, meta_ref, picked_ref, scaled, aligned, one_far, one_near, two_far, two_near, meta_one, meta_two, part, landed, gathered, work, upper,
+    z_send, z_recv, x_send, x_recv, meta_send, meta_recv, own_sem,
     sum_send, sum_recv, all_send, all_recv,
 ):
     rows = a_ref.shape[0]
     tile = rows // 2
     half = tile // 2
-    piece = rows // PIECES
-    per_block = PIECES // 2
+    piece = tile // 4
+    far_pieces = [(n * piece, piece) for n in range(4)]
+    near_pieces = far_pieces[:3] + [
+        (3 * piece, piece // 2), (3 * piece + piece // 2, piece // 2)]
+    per_block = len(far_pieces)
+    pieces = far_pieces + near_pieces
+    count = len(pieces)
     group = lax.axis_index("blk")
     slab = lax.axis_index("slab")
     chip = slab // 2
@@ -103,20 +108,39 @@
     far = 1 - chip
     near = chip
 
+    own_copy = pltpu.make_async_copy(a_ref, own, own_sem.at[0])
+    own_copy.start()
     barrier = pltpu.get_barrier_semaphore()
     for other in (ahead, behind, across):
         pl.semaphore_signal(barrier, inc=1, device_id=(other, slab), device_id_type=MESH)
     for other in peers:
         pl.semaphore_signal(barrier, inc=1, device_id=(group, other), device_id_type=MESH)
+    for i in range(2):
+        live = jnp.full((1, half), counts_ref[i, 0], jnp.int32)
+        for m in range(slots):
+            column = jnp.full((1, half), cols_ref[i, 0, m], jnp.int32)
+            meta_ref[i * slots + m:i * slots + m + 1, :] = jnp.where(live > m, column, -1)
+    entries = meta_ref[...]
+    for h in range(2):
+        factors = jnp.zeros((2 * slots, half), jnp.float32)
+        for c in range(scal_ref.shape[0] // 2):
+            factors = jnp.where(entries == c, scal_ref[2 * c + h:2 * c + h + 1, :], factors)
+        picked_ref[:, h * half:(h + 1) * half] = factors
     pl.semaphore_wait(barrier, 6)
 
     def piece_rows(n):
-        block = far if n < per_block else near
-        return pl.ds(pl.multiple_of(block * tile + (n % per_block) * piece, piece), piece)
+        offset, size = pieces[n]
+        if n < per_block:
+            start = far * tile + offset
+        elif offset < half:
+            start = near * tile + (1 - core) * half + offset
+        else:
+            start = near * tile + core * half + offset - half
+        return pl.ds(pl.multiple_of(start, size), size)
 
     def piece_of(far_ref, near_ref, n):
-        start = n % per_block * piece
-        return (far_ref if n < per_block else near_ref).at[start:start + piece]
+        offset, size = pieces[n]
+        return (far_ref if n < per_block else near_ref).at[offset:offset + size]
 
     def to_ahead(n):
         return pltpu.make_async_remote_copy(
@@ -141,20 +165,21 @@
             device_id=(across, slab), device_id_type=MESH)
 
     meta_ahead().start()
-    for n in range(PIECES):
+    for n in range(count):
         to_ahead(n).start()
 
     @pl.when(odd == 0)
     def _():
         meta_across(meta_ref).start()
-        for n in range(PIECES):
+        for n in range(count):
             to_across(n, a_ref.at[piece_rows(n)]).start()
 
     def scale_slot(i, m):
         where = (pl.ds(i * tile, tile), pl.ds(m * tile, tile))
         factors = picked_ref[i * slots + m:i * slots + m + 1, :]
-        scaled[where] = (a_ref[where].astype(jnp.float32) * factors).astype(jnp.bfloat16)
-
+        scaled[where] = (own[where].astype(jnp.float32) * factors).astype(jnp.bfloat16)
+
+    own_copy.wait()
     for i in range(2):
         for m in range(slots):
             scale_slot(i, m)
@@ -165,25 +190,23 @@
             send_sem=sum_send.at[plane, d], recv_sem=sum_recv.at[plane, d],
             device_id=(group, peers[d]), device_id_type=MESH)
 
-    def multiply(plane, block, source, other_meta):
-        first = pl.ds(0, tile)
-        if plane == 0:
-            first = pl.ds(pl.multiple_of(block * tile, tile), tile)
+    def multiply(plane, block, source, start, size, other_meta, targets):
+        first = pl.ds(start, size)
 
         def align(i):
             def one_slot(m, carry):
                 mine = meta_ref[pl.ds(i * slots + m, 1), :]
-                total = jnp.zeros((tile, tile), jnp.bfloat16)
+                total = jnp.zeros((size, tile), jnp.bfloat16)
                 for n in range(slots):
                     theirs = other_meta[pl.ds(block * slots + n, 1), :]
                     same = jnp.where(mine == theirs, jnp.float32(1.0), jnp.float32(0.0))
                     same = jnp.concatenate([same, same], axis=1).astype(jnp.bfloat16)
                     total += source[first, n * tile:(n + 1) * tile] * same
-                aligned[:, pl.ds(pl.multiple_of(m * tile, tile), tile)] = total
+                aligned[:size, pl.ds(pl.multiple_of(m * tile, tile), tile)] = total
                 return carry
 
             lax.fori_loop(0, slots, one_slot, 0)
-            return aligned[...]
+            return aligned[:size]
 
         def one(i, direct):
             here = pl.ds(pl.multiple_of(i * tile, tile), tile)
@@ -191,22 +214,33 @@
             total = lax.dot_general(
                 scaled[here, :], other, (((1,), (1,)), ((), ())),
                 preferred_element_type=jnp.float32)
-            part[plane, 2 * block, here] = total[:, :half]
-            part[plane, 2 * block + 1, here] = total[:, half:]
+            if size == half:
+                part[plane, 2 * block + (start_owner(targets)), here] = total
+            else:
+                part[plane, 2 * block, here] = total[:, :half]
+                part[plane, 2 * block + 1, here] = total[:, half:]
 
         one(block, plane == 0)
         one(1 - block, False)
-        if block is far:
-            sum_copy(plane, 1).start()
-            sum_copy(plane, 2).start()
-        else:
-            sum_copy(plane, 0).start()
+        for d in targets:
+            sum_copy(plane, d).start()
+
+    def start_owner(targets):
+        return 1 - core if targets else core
+
+    def multiply_far(plane, source, other_meta):
+        multiply(plane, far, source, 0, tile, other_meta, (1, 2))
+
+    def multiply_mate(plane, source, other_meta):
+        multiply(plane, near, source, 0, half, other_meta, (0,))
+
+    def multiply_own(plane, source, other_meta):
+        multiply(plane, near, source, half, half, other_meta, ())
 
     def near_copies(n):
         here = pl.ds(pl.multiple_of((n - per_block) * piece, piece), piece)
-        there = pl.ds(pl.multiple_of(near * tile + (n - per_block) * piece, piece), piece)
         incoming = pltpu.make_async_remote_copy(
-            src_ref=a_ref.at[there], dst_ref=two_near.at[here],
+            src_ref=a_ref.at[pl.ds(0, piece)], dst_ref=two_near.at[here],
             send_sem=z_send.at[n], recv_sem=z_recv.at[n],
             device_id=(ahead, slab), device_id_type=MESH)
         outgoing = pltpu.make_async_remote_copy(
@@ -230,8 +264,10 @@
         def _():
             to_across(n, piece_of(two_far, two_near, n)).start()
 
-    multiply(0, far, a_ref, meta_ref)
-    multiply(0, near, a_ref, meta_ref)
+    far_rows = pl.multiple_of(far * tile, tile)
+    near_rows = pl.multiple_of(near * tile, tile)
+    multiply(0, far, own, far_rows, tile, meta_ref, (1, 2))
+    multiply(0, near, own, near_rows, tile, meta_ref, (0,))
 
     meta_ahead().wait_recv()
 
@@ -241,6 +277,7 @@
 
     forward(0)
     meta_across(meta_ref).wait_recv()
+    forward(1)
 
     for d in range(3):
         sum_copy(0, d).wait_recv()
@@ -249,27 +286,31 @@
     ridge = jnp.where(row_ids == col_ids, jnp.float32(ridge_shift), jnp.float32(0.0))
     gathered[slab] = (part[0, slab] + landed[0, 0]) + (landed[0, 1] + landed[0, 2]) + ridge
 
+    sent = (slab, slab, facing)
+
     def all_copy(d):
         return pltpu.make_async_remote_copy(
-            src_ref=gathered.at[slab], dst_ref=gathered.at[slab],
+            src_ref=gathered.at[sent[d]], dst_ref=gathered.at[sent[d]],
             send_sem=all_send.at[d], recv_sem=all_recv.at[d],
-            device_id=(group, peers[d]), device_id_type=MESH)
+            device_id=(group, (mate, facing, mate)[d]), device_id_type=MESH)
 
     def all_arrival(d):
         return pltpu.make_async_remote_copy(
-            src_ref=gathered.at[slab], dst_ref=gathered.at[peers[d]],
+            src_ref=gathered.at[sent[d]], dst_ref=gathered.at[peers[d]],
             send_sem=all_send.at[d], recv_sem=all_recv.at[d],
-            device_id=(group, peers[d]), device_id_type=MESH)
-
-    for d in (1, 2, 0):
-        all_copy(d).start()
-
-    for n in range(1, per_block):
+            device_id=(group, (mate, facing, mate)[d]), device_id_type=MESH)
+
+    all_copy(1).start()
+    all_copy(0).start()
+
+    for n in range(2, per_block):
         forward(n)
-    multiply(2, far, two_far, meta_two)
-    for d in range(3):
-        all_arrival(d).wait_recv()
-    pivot = pos_ref[0:1, :]
+    all_arrival(1).wait_recv()
+    all_copy(2).start()
+    multiply_far(2, two_far, meta_two)
+    all_arrival(0).wait_recv()
+    all_arrival(2).wait_recv()
+    pivot = jnp.full((1, half), panel_ref[0], jnp.int32)
     first = (pivot & 1) == 0
     pivot_tile = jnp.concatenate(
         [jnp.where(first, gathered[h, :tile], gathered[2 + h, tile:]) for h in range(2)], axis=1)
@@ -296,7 +337,11 @@
         def _():
             for p in range(per_block):
                 to_across(p, piece_of(two_far, two_near, p)).wait_recv()
-            multiply(1, far, one_far, meta_one)
+            multiply_far(1, one_far, meta_one)
+
+        @pl.when(n == 2)
+        def _():
+            multiply_mate(2, two_near, meta_two)
 
         return carry
 
@@ -317,11 +362,15 @@
     band_ref[0, :tile] = jnp.where(holds, new_top, top)
     band_ref[0, tile:] = jnp.where(holds, new_low, low)
 
-    forward(PIECES - 1)
-    multiply(2, near, two_near, meta_two)
-    for n in range(per_block, PIECES):
+    forward(count - 2)
+    forward(count - 1)
+    for n in (per_block, per_block + 1):
         to_across(n, piece_of(two_far, two_near, n)).wait_recv()
-    multiply(1, near, one_near, meta_one)
+    multiply_mate(1, one_near, meta_one)
+    multiply_own(2, two_near, meta_two)
+    for n in range(per_block + 2, count):
+        to_across(n, piece_of(two_far, two_near, n)).wait_recv()
+    multiply_own(1, one_near, meta_one)
     for plane in (2, 1):
         for d in range(3):
             sum_copy(plane, d).wait_recv()
@@ -330,7 +379,7 @@
 
     meta_ahead().wait_send()
     meta_across(meta_ref).wait_send()
-    for n in range(PIECES):
+    for n in range(count):
         to_ahead(n).wait_send()
         to_across(n, piece_of(two_far, two_near, n)).wait_send()
     for d in range(3):
@@ -345,24 +394,19 @@
     slots = tile_cols.shape[2]
     tile = rows // blocks_here
     half = rows // 4
-    col_tiles = scaling.shape[0] // tile
     groups = lax.axis_size("blk")
-    cols = tile_cols[:, 0, :]
-    slot_ids = jnp.arange(slots, dtype=jnp.int32)
-    live = slot_ids[None, :] < tile_counts
-    picked = jnp.where(live[..., None], scaling.reshape(col_tiles, tile)[cols], jnp.float32(0.0))
-    picked = picked.reshape(blocks_here * slots, tile)
-    meta = jnp.where(live, cols, -1).reshape(blocks_here * slots, 1)
-    meta = jnp.broadcast_to(meta, (blocks_here * slots, half))
-    positions = jnp.full((8, half), panel[0], jnp.int32)
     vmem = pl.BlockSpec(memory_space=pltpu.VMEM)
+    smem = pl.BlockSpec(memory_space=pltpu.SMEM)
     dma = pltpu.SemaphoreType.DMA
     band = pl.pallas_call(
         functools.partial(band_kernel, groups, slots),
         out_shape=jax.ShapeDtypeStruct((3, rows, half), jnp.float32),
-        in_specs=[vmem] * 4,
+        in_specs=[pl.BlockSpec(memory_space=pl.ANY), smem, smem, vmem, smem],
         out_specs=vmem,
         scratch_shapes=[
+            pltpu.VMEM(a_tiles.shape, jnp.bfloat16),
+            pltpu.VMEM((2 * slots, half), jnp.int32),
+            pltpu.VMEM((2 * slots, tile), jnp.float32),
             pltpu.VMEM(a_tiles.shape, jnp.bfloat16),
             pltpu.VMEM((tile, slots * tile), jnp.bfloat16),
             *[pltpu.VMEM((tile, slots * tile), jnp.bfloat16)] * 4,
@@ -373,13 +417,13 @@
             pltpu.VMEM((tile, 2 * tile), jnp.float32),
             pltpu.VMEM((tile, 2 * tile), jnp.float32),
             dma((PIECES,)), dma((PIECES,)), dma((PIECES,)), dma((PIECES,)),
-            dma((2,)), dma((2,)),
+            dma((2,)), dma((2,)), dma((1,)),
             dma((3, 3)), dma((3, 3)), dma((3,)), dma((3,)),
         ],
         compiler_params=pltpu.CompilerParams(
-            collective_id=0, has_side_effects=True, vmem_limit_bytes=40 * 2**20),
+            collective_id=0, has_side_effects=True, vmem_limit_bytes=60 * 2**20),
         name="band",
-    )(a_tiles, picked, meta, positions)
+    )(a_tiles, tile_cols, tile_counts, scaling.reshape(-1, half), panel)
 
     return jnp.transpose(band, (1, 0, 2))
 

time: 74.8 us -> 69.4 us (0.928)
  other arithmetic: 2.84 us -> 0 us
  Pallas kernels: 66.4 us -> 65.1 us
  local copies, waits for them, and re-layouts: 4.61 us -> 3.36 us
    unnamed x1 -> x0, other arithmetic: 1.34 us -> none
    pallas_call x1, Pallas kernels: 66.4 us -> 65.1 us  [body(): pl.pallas_call(functools.partial(band_kernel, groups, slots), out_shape=j...]
    select_n x3 -> x0, other arithmetic: 0.76 us -> none  [the longest x1 0.68 us: body(): scaling.reshape(col_tiles, tile)[cols]]
    unnamed x4 -> x2, local copies, waits for them, and re-layouts: 2.99 us -> 3.36 us
where the time goes in v3:
time: 69.4 us; the launch traced here: 69.1 us
  Pallas kernels  65.1 us (94%)
  local copies, waits for them, and re-layouts  3.36 us (5%)
    pallas_call x1, Pallas kernels, body(): pl.pallas_call(functools.partial(band_kernel, groups, slots), out_shape=j...  65.1 us
    unnamed x2, local copies, waits for them, and re-layouts  3.36 us

profile of v3, /device:TPU:0, one launch (start us, length us, event | category | flops | bytes accessed | tf_op | source)
XLA Modules:
  0.0 69.1 jit_solution(4256243718263373869)
XLA Ops:
  0.7 1.3 %copy.6.counts_ref = s32[2,1]{1,0:T(2,128)} copy(s32[2,1]{0,1:T(1,128)} %param.7) | data formatting | bytes 16 | tf_op args[2]
  1.9 65.1 %band.1 = f32[3,512,128]{2,1,0:T(8,128)} custom-call(bf16[512,2048]{1,0:T(8,128)(2,1)} %a_ref.1, s32[2,1,8]{2,1,0:T(1,128)} %cols_ref.1, s32[2,1]{1,0:T(2,128)} %copy.6.counts_ref, f32[32,128]{1,0:T(8,128)} %bitcast.3, s32[1]{0:T(128)S(6)} %copy.8.panel_ref), custom_call_target="tpu_custom_call" | custom-call | tf_op jit(solution)/shard_map/band/pallas_call | solution.py:401
  67.1 2.1 %copy.9 = f32[512,3,128]{2,0,1:T(8,128)} copy(f32[512,3,128]{2,0,1:T(8,128)} %bitcast.2) | data formatting | bytes 1572864

commit v4 on v3

--- a/solution.py
+++ b/solution.py
@@ -9,7 +9,7 @@
 
 ridge_shift = 0.05
 MESH = pl.DeviceIdType.MESH
-PIECES = 9
+PIECES = 16
 STRIP = 32
 
 
@@ -79,20 +79,15 @@
 
 def band_kernel(
     groups, slots, a_ref, cols_ref, counts_ref, scal_ref, panel_ref, band_ref,
-    own, meta_ref, picked_ref, scaled, aligned, one_far, one_near, two_far, two_near, meta_one, meta_two, part, landed, gathered, work, upper,
+    own, meta_ref, picked_ref, scaled, aligned, a_one, a_two, meta_one, meta_two, part, landed, gathered, work, upper,
     z_send, z_recv, x_send, x_recv, meta_send, meta_recv, own_sem,
     sum_send, sum_recv, all_send, all_recv,
 ):
     rows = a_ref.shape[0]
     tile = rows // 2
     half = tile // 2
-    piece = tile // 4
-    far_pieces = [(n * piece, piece) for n in range(4)]
-    near_pieces = far_pieces[:3] + [
-        (3 * piece, piece // 2), (3 * piece + piece // 2, piece // 2)]
-    per_block = len(far_pieces)
-    pieces = far_pieces + near_pieces
-    count = len(pieces)
+    piece = rows // PIECES
+    per_unit = PIECES // 4
     group = lax.axis_index("blk")
     slab = lax.axis_index("slab")
     chip = slab // 2
@@ -116,7 +111,7 @@
     for other in peers:
         pl.semaphore_signal(barrier, inc=1, device_id=(group, other), device_id_type=MESH)
     for i in range(2):
-        live = jnp.full((1, half), counts_ref[i, 0], jnp.int32)
+        live = jnp.full((1, half), counts_ref[i], jnp.int32)
         for m in range(slots):
             column = jnp.full((1, half), cols_ref[i, 0, m], jnp.int32)
             meta_ref[i * slots + m:i * slots + m + 1, :] = jnp.where(live > m, column, -1)
@@ -128,32 +123,30 @@
         picked_ref[:, h * half:(h + 1) * half] = factors
     pl.semaphore_wait(barrier, 6)
 
+    units = ((far, core, (1,)), (far, 1 - core, (2,)), (near, 1 - core, (0,)), (near, core, ()))
+
     def piece_rows(n):
-        offset, size = pieces[n]
-        if n < per_block:
-            start = far * tile + offset
-        elif offset < half:
-            start = near * tile + (1 - core) * half + offset
-        else:
-            start = near * tile + core * half + offset - half
-        return pl.ds(pl.multiple_of(start, size), size)
-
-    def piece_of(far_ref, near_ref, n):
-        offset, size = pieces[n]
-        return (far_ref if n < per_block else near_ref).at[offset:offset + size]
-
-    def to_ahead(n):
-        return pltpu.make_async_remote_copy(
-            src_ref=a_ref.at[piece_rows(n)], dst_ref=piece_of(two_far, two_near, n),
+        block, side, _ = units[n // per_unit]
+        start = block * tile + side * half + n % per_unit * piece
+        return pl.ds(pl.multiple_of(start, piece), piece)
+
+    def landing(n):
+        return pl.ds(pl.multiple_of(n * piece, piece), piece)
+
+    def to_ahead(n, source):
+        return pltpu.make_async_remote_copy(
+            src_ref=source, dst_ref=a_two.at[landing(n)],
             send_sem=z_send.at[n], recv_sem=z_recv.at[n],
             device_id=(ahead, slab), device_id_type=MESH)
 
     def to_across(n, source):
         return pltpu.make_async_remote_copy(
-            src_ref=source, dst_ref=piece_of(one_far, one_near, n),
+            src_ref=source, dst_ref=a_one.at[landing(n)],
             send_sem=x_send.at[n], recv_sem=x_recv.at[n],
             device_id=(across, slab), device_id_type=MESH)
 
+    some_piece = a_ref.at[pl.ds(0, piece)]
+
     def meta_ahead():
         return pltpu.make_async_remote_copy(
             src_ref=meta_ref, dst_ref=meta_two, send_sem=meta_send.at[0], recv_sem=meta_recv.at[0],
@@ -165,13 +158,13 @@
             device_id=(across, slab), device_id_type=MESH)
 
     meta_ahead().start()
-    for n in range(count):
-        to_ahead(n).start()
+    for n in range(PIECES):
+        to_ahead(n, a_ref.at[piece_rows(n)]).start()
 
     @pl.when(odd == 0)
     def _():
         meta_across(meta_ref).start()
-        for n in range(count):
+        for n in range(PIECES):
             to_across(n, a_ref.at[piece_rows(n)]).start()
 
     def scale_slot(i, m):
@@ -190,7 +183,7 @@
             send_sem=sum_send.at[plane, d], recv_sem=sum_recv.at[plane, d],
             device_id=(group, peers[d]), device_id_type=MESH)
 
-    def multiply(plane, block, source, start, size, other_meta, targets):
+    def multiply(plane, block, source, start, size, other_meta, targets, side):
         first = pl.ds(start, size)
 
         def align(i):
@@ -215,7 +208,7 @@
                 scaled[here, :], other, (((1,), (1,)), ((), ())),
                 preferred_element_type=jnp.float32)
             if size == half:
-                part[plane, 2 * block + (start_owner(targets)), here] = total
+                part[plane, 2 * block + side, here] = total
             else:
                 part[plane, 2 * block, here] = total[:, :half]
                 part[plane, 2 * block + 1, here] = total[:, half:]
@@ -225,50 +218,24 @@
         for d in targets:
             sum_copy(plane, d).start()
 
-    def start_owner(targets):
-        return 1 - core if targets else core
-
-    def multiply_far(plane, source, other_meta):
-        multiply(plane, far, source, 0, tile, other_meta, (1, 2))
-
-    def multiply_mate(plane, source, other_meta):
-        multiply(plane, near, source, 0, half, other_meta, (0,))
-
-    def multiply_own(plane, source, other_meta):
-        multiply(plane, near, source, half, half, other_meta, ())
-
-    def near_copies(n):
-        here = pl.ds(pl.multiple_of((n - per_block) * piece, piece), piece)
-        incoming = pltpu.make_async_remote_copy(
-            src_ref=a_ref.at[pl.ds(0, piece)], dst_ref=two_near.at[here],
-            send_sem=z_send.at[n], recv_sem=z_recv.at[n],
-            device_id=(ahead, slab), device_id_type=MESH)
-        outgoing = pltpu.make_async_remote_copy(
-            src_ref=two_near.at[here], dst_ref=one_near.at[here],
-            send_sem=x_send.at[n], recv_sem=x_recv.at[n],
-            device_id=(across, slab), device_id_type=MESH)
-        return incoming, outgoing
-
-    def forward_near(n):
-        incoming, outgoing = near_copies(n)
-        incoming.wait_recv()
+    def multiply_unit(plane, u):
+        source, other_meta = ((a_one, meta_one), (a_two, meta_two))[plane - 1]
+        block, side, targets = units[u]
+        if plane == 1:
+            for n in range(u * per_unit, (u + 1) * per_unit):
+                to_across(n, some_piece).wait_recv()
+        multiply(plane, block, source, u * half, half, other_meta, targets, side)
+
+    def forward(n):
+        to_ahead(n, some_piece).wait_recv()
 
         @pl.when(odd == 1)
         def _():
-            outgoing.start()
-
-    def forward(n):
-        to_ahead(n).wait_recv()
-
-        @pl.when(odd == 1)
-        def _():
-            to_across(n, piece_of(two_far, two_near, n)).start()
+            to_across(n, a_two.at[landing(n)]).start()
 
     far_rows = pl.multiple_of(far * tile, tile)
     near_rows = pl.multiple_of(near * tile, tile)
-    multiply(0, far, own, far_rows, tile, meta_ref, (1, 2))
-    multiply(0, near, own, near_rows, tile, meta_ref, (0,))
-
+    multiply(0, far, own, far_rows, tile, meta_ref, (1, 2), 0)
     meta_ahead().wait_recv()
 
     @pl.when(odd == 1)
@@ -276,9 +243,11 @@
         meta_across(meta_two).start()
 
     forward(0)
+    multiply(0, near, own, near_rows, tile, meta_ref, (0,), 0)
+    for n in (1, 2, 3):
+        forward(n)
+    multiply_unit(2, 0)
     meta_across(meta_ref).wait_recv()
-    forward(1)
-
     for d in range(3):
         sum_copy(0, d).wait_recv()
     row_ids = lax.broadcasted_iota(jnp.int32, (rows, half), 0)
@@ -303,11 +272,15 @@
     all_copy(1).start()
     all_copy(0).start()
 
-    for n in range(2, per_block):
-        forward(n)
+    forward(4)
+    forward(5)
+    multiply_unit(1, 0)
+    forward(6)
     all_arrival(1).wait_recv()
     all_copy(2).start()
-    multiply_far(2, two_far, meta_two)
+    forward(7)
+    multiply_unit(2, 1)
+    forward(8)
     all_arrival(0).wait_recv()
     all_arrival(2).wait_recv()
     pivot = jnp.full((1, half), panel_ref[0], jnp.int32)
@@ -320,32 +293,29 @@
     work[:, tile:] = other_tile.T
 
     strips = tile // STRIP
-    quarter = strips // per_block
-
-    def some_strips(n, carry):
-        def one_strip(s, carry):
-            factor_strip(work, upper, s)
-            return carry
-
-        lax.fori_loop(n * quarter, (n + 1) * quarter, one_strip, 0)
-
-        @pl.when(n < per_block - 1)
+
+    def one_strip(s, carry):
+        factor_strip(work, upper, s)
+
+        @pl.when(s < strips - 1)
         def _():
-            forward_near(n + per_block)
-
-        @pl.when(n == 1)
+            forward(s + PIECES - strips + 1)
+
+        @pl.when(s == 1)
         def _():
-            for p in range(per_block):
-                to_across(p, piece_of(two_far, two_near, p)).wait_recv()
-            multiply_far(1, one_far, meta_one)
-
-        @pl.when(n == 2)
+            multiply_unit(1, 1)
+
+        @pl.when(s == 3)
         def _():
-            multiply_mate(2, two_near, meta_two)
+            multiply_unit(2, 2)
+
+        @pl.when(s == 5)
+        def _():
+            multiply_unit(1, 2)
 
         return carry
 
-    lax.fori_loop(0, per_block, some_strips, 0)
+    lax.fori_loop(0, strips, one_strip, 0)
 
     lower_half = upper[pl.ds(pl.multiple_of(core * half, half), half), :].T
     other_half = upper[:, pl.ds(pl.multiple_of(tile + core * half, half), half)]
@@ -362,15 +332,8 @@
     band_ref[0, :tile] = jnp.where(holds, new_top, top)
     band_ref[0, tile:] = jnp.where(holds, new_low, low)
 
-    forward(count - 2)
-    forward(count - 1)
-    for n in (per_block, per_block + 1):
-        to_across(n, piece_of(two_far, two_near, n)).wait_recv()
-    multiply_mate(1, one_near, meta_one)
-    multiply_own(2, two_near, meta_two)
-    for n in range(per_block + 2, count):
-        to_across(n, piece_of(two_far, two_near, n)).wait_recv()
-    multiply_own(1, one_near, meta_one)
+    multiply_unit(2, 3)
+    multiply_unit(1, 3)
     for plane in (2, 1):
         for d in range(3):
             sum_copy(plane, d).wait_recv()
@@ -379,9 +342,9 @@
 
     meta_ahead().wait_send()
     meta_across(meta_ref).wait_send()
-    for n in range(count):
-        to_ahead(n).wait_send()
-        to_across(n, piece_of(two_far, two_near, n)).wait_send()
+    for n in range(PIECES):
+        to_ahead(n, some_piece).wait_send()
+        to_across(n, some_piece).wait_send()
     for d in range(3):
         all_copy(d).wait_send()
         for plane in range(3):
@@ -409,7 +372,7 @@
             pltpu.VMEM((2 * slots, tile), jnp.float32),
             pltpu.VMEM(a_tiles.shape, jnp.bfloat16),
             pltpu.VMEM((tile, slots * tile), jnp.bfloat16),
-            *[pltpu.VMEM((tile, slots * tile), jnp.bfloat16)] * 4,
+            *[pltpu.VMEM(a_tiles.shape, jnp.bfloat16)] * 2,
             *[pltpu.VMEM((blocks_here * slots, half), jnp.int32)] * 2,
             pltpu.VMEM((3, 4, rows, half), jnp.float32),
             pltpu.VMEM((3, 3, rows, half), jnp.float32),
@@ -421,9 +384,9 @@
             dma((3, 3)), dma((3, 3)), dma((3,)), dma((3,)),
         ],
         compiler_params=pltpu.CompilerParams(
-            collective_id=0, has_side_effects=True, vmem_limit_bytes=60 * 2**20),
+            collective_id=0, has_side_effects=True, vmem_limit_bytes=52 * 2**20),
         name="band",
-    )(a_tiles, tile_cols, tile_counts, scaling.reshape(-1, half), panel)
+    )(a_tiles, tile_cols, tile_counts.reshape(-1), scaling.reshape(-1, half), panel)
 
     return jnp.transpose(band, (1, 0, 2))
 

time: 69.4 us -> 68.8 us (level)
    unnamed x2 -> x7, local copies, waits for them, and re-layouts: 3.36 us -> 2.93 us
where the time goes in v4:
time: 68.8 us; the launch traced here: 68.5 us
  Pallas kernels  64.9 us (94%)
  local copies, waits for them, and re-layouts  2.93 us (4%)
    pallas_call x1, Pallas kernels, body(): pl.pallas_call(functools.partial(band_kernel, groups, slots), out_shape=j...  64.9 us
    unnamed x7, local copies, waits for them, and re-layouts  2.93 us

profile of v4, /device:TPU:0, one launch (start us, length us, event | category | flops | bytes accessed | tf_op | source)
XLA Modules:
  0.0 68.5 jit_solution(17352301667566284057)
XLA Ops:
  0.7 0.0 copy-start
  0.7 0.7 %copy-done = f32[4096]{0:T(1024)S(1)} copy-done((f32[4096]{0:T(1024)S(1)}, f32[4096]{0:T(1024)}, u32[]{:S(2)}) %copy-start) | copy-done | bytes 16408
  1.4 0.0 copy-start.1
  1.4 0.7 copy-done.1
  2.0 0.0 copy-start.2
  2.1 0.7 copy-done.2
  2.7 64.9 %band.1 = f32[3,512,128]{2,1,0:T(8,128)S(1)} custom-call(bf16[512,2048]{1,0:T(8,128)(2,1)} %a_ref.1, s32[2,1,8]{2,1,0:T(1,128)S(1)} %copy-done.1, s32[2]{0:T(128)S(1)} %bitcast.5, f32[32,128]{1,0:T(8,128)S(1)} %bitcast.4, s32[1]{0:T(128)S(6)} %copy.7.panel_ref), custom_call_target="tpu_custom_call" | custom-call | tf_op jit(solution)/shard_map/band/pallas_call | solution.py:364
  67.7 0.9 %copy.8 = f32[512,3,128]{2,0,1:T(8,128)} copy(f32[512,3,128]{2,0,1:T(8,128)S(1)} %bitcast.3) | data formatting | bytes 1572864
Async XLA Ops:
  0.7 0.7 %copy-start = (f32[4096]{0:T(1024)S(1)}, f32[4096]{0:T(1024)}, u32[]{:S(2)}) copy-start(f32[4096]{0:T(1024)} %param.8) | copy-start | bytes 49156
  1.4 0.7 copy-start.1
  2.0 0.7 copy-start.2

commit v5 on v4

--- a/solution.py
+++ b/solution.py
@@ -74,7 +74,10 @@
     own = lax.broadcasted_iota(jnp.int32, rows.shape, 0) + start
     rows = jnp.where(lanes >= own, rows, jnp.float32(0.0))
     upper[pl.ds(start, STRIP), :] = rows
-    work[...] -= transposed_product(rows[:, :size], rows)
+
+    @pl.when(s < size // STRIP - 1)
+    def _():
+        work[...] -= transposed_product(rows[:, :size], rows)
 
 
 def band_kernel(
@@ -295,12 +298,12 @@
     strips = tile // STRIP
 
     def one_strip(s, carry):
-        factor_strip(work, upper, s)
-
         @pl.when(s < strips - 1)
         def _():
             forward(s + PIECES - strips + 1)
 
+        factor_strip(work, upper, s)
+
         @pl.when(s == 1)
         def _():
             multiply_unit(1, 1)
@@ -308,10 +311,6 @@
         @pl.when(s == 3)
         def _():
             multiply_unit(2, 2)
-
-        @pl.when(s == 5)
-        def _():
-            multiply_unit(1, 2)
 
         return carry
 
@@ -332,6 +331,7 @@
     band_ref[0, :tile] = jnp.where(holds, new_top, top)
     band_ref[0, tile:] = jnp.where(holds, new_low, low)
 
+    multiply_unit(1, 2)
     multiply_unit(2, 3)
     multiply_unit(1, 3)
     for plane in (2, 1):
@@ -384,7 +384,7 @@
             dma((3, 3)), dma((3, 3)), dma((3,)), dma((3,)),
         ],
         compiler_params=pltpu.CompilerParams(
-            collective_id=0, has_side_effects=True, vmem_limit_bytes=52 * 2**20),
+            collective_id=0, has_side_effects=True, vmem_limit_bytes=60 * 2**20),
         name="band",
     )(a_tiles, tile_cols, tile_counts.reshape(-1), scaling.reshape(-1, half), panel)
 

time: 68.8 us -> 68.4 us (level)
  local copies, waits for them, and re-layouts: 2.93 us -> 2.06 us
    unnamed x7 -> x1, local copies, waits for them, and re-layouts: 2.93 us -> 2.06 us
where the time goes in v5:
time: 68.4 us; the launch traced here: 68.2 us
  Pallas kernels  65.5 us (96%)
  local copies, waits for them, and re-layouts  2.06 us (3%)
    pallas_call x1, Pallas kernels, body(): pl.pallas_call(functools.partial(band_kernel, groups, slots), out_shape=j...  65.5 us
    unnamed x1, local copies, waits for them, and re-layouts  2.06 us

profile of v5, /device:TPU:0, one launch (start us, length us, event | category | flops | bytes accessed | tf_op | source)
XLA Modules:
  0.0 68.2 jit_solution(10279307947988107206)
XLA Ops:
  0.7 65.5 %band.1 = f32[3,512,128]{2,1,0:T(8,128)} custom-call(bf16[512,2048]{1,0:T(8,128)(2,1)} %a_ref.1, s32[2,1,8]{2,1,0:T(1,128)} %cols_ref.1, s32[2]{0:T(128)} %bitcast.5, f32[32,128]{1,0:T(8,128)} %bitcast.4, s32[1]{0:T(128)S(6)} %copy.7.panel_ref), custom_call_target="tpu_custom_call" | custom-call | tf_op jit(solution)/shard_map/band/pallas_call | solution.py:364
  66.1 2.1 %copy.8 = f32[512,3,128]{2,0,1:T(8,128)} copy(f32[512,3,128]{2,0,1:T(8,128)} %bitcast.3) | data formatting | bytes 1572864

commit v6 on v5

--- a/solution.py
+++ b/solution.py
@@ -298,12 +298,12 @@
     strips = tile // STRIP
 
     def one_strip(s, carry):
+        factor_strip(work, upper, s)
+
         @pl.when(s < strips - 1)
         def _():
             forward(s + PIECES - strips + 1)
 
-        factor_strip(work, upper, s)
-
         @pl.when(s == 1)
         def _():
             multiply_unit(1, 1)
@@ -311,6 +311,10 @@
         @pl.when(s == 3)
         def _():
             multiply_unit(2, 2)
+
+        @pl.when(s == 5)
+        def _():
+            multiply_unit(1, 2)
 
         return carry
 
@@ -331,7 +335,6 @@
     band_ref[0, :tile] = jnp.where(holds, new_top, top)
     band_ref[0, tile:] = jnp.where(holds, new_low, low)
 
-    multiply_unit(1, 2)
     multiply_unit(2, 3)
     multiply_unit(1, 3)
     for plane in (2, 1):

time: 68.4 us -> 69 us (level)
  no operation moved by 1% of the time
where the time goes in v6:
time: 69 us; the launch traced here: 68.7 us
  Pallas kernels  66 us (96%)
  local copies, waits for them, and re-layouts  2.06 us (3%)
    pallas_call x1, Pallas kernels, body(): pl.pallas_call(functools.partial(band_kernel, groups, slots), out_shape=j...  66 us
    unnamed x1, local copies, waits for them, and re-layouts  2.06 us

profile of v6, /device:TPU:0, one launch (start us, length us, event | category | flops | bytes accessed | tf_op | source)
XLA Modules:
  0.0 68.7 jit_solution(1194352862074552009)
XLA Ops:
  0.7 66.0 %band.1 = f32[3,512,128]{2,1,0:T(8,128)} custom-call(bf16[512,2048]{1,0:T(8,128)(2,1)} %a_ref.1, s32[2,1,8]{2,1,0:T(1,128)} %cols_ref.1, s32[2]{0:T(128)} %bitcast.5, f32[32,128]{1,0:T(8,128)} %bitcast.4, s32[1]{0:T(128)S(6)} %copy.7.panel_ref), custom_call_target="tpu_custom_call" | custom-call | tf_op jit(solution)/shard_map/band/pallas_call | solution.py:367
  66.7 2.1 %copy.8 = f32[512,3,128]{2,0,1:T(8,128)} copy(f32[512,3,128]{2,0,1:T(8,128)} %bitcast.3) | data formatting | bytes 1572864
